TPU v7x, 32 devices: a whole 2x2x4 slice. The times are simulated.
32 devices in a mesh: rep: 8 (over z, y), fsdp: 4 (over x, core).
Axes of the slice: x: 2, y: 2, z: 4, core: 2. Of those that a mesh axis runs over, the one named last changes fastest.
Arguments:
- hidden: bfloat16 [8, 1024, 4096], P('rep', 'fsdp'), may hold values from -6 to 6
- key_grad: bfloat16 [8, 1024, 512], P('rep', 'fsdp'), may hold values from -0.1875 to 0.1875
- weight: float32 [8, 4096, 512], P('rep', 'fsdp'), may hold values from -0.09375 to 0.09375
- moment1: bfloat16 [8, 4096, 512], P('rep', 'fsdp'), may hold values from -3 to 3
- moment2: bfloat16 [8, 4096, 512], P('rep', 'fsdp'), may hold values from 0.19921875 to 2
- step: int32 [], replicated, may hold values from 0 to 999
Outputs:
- keys: bfloat16 [8, 1024, 512], P('rep', 'fsdp')
- input_grad: bfloat16 [8, 1024, 4096], P('rep', 'fsdp')
- weight_next: float32 [8, 4096, 512], P('rep', 'fsdp')
- moment1_next: bfloat16 [8, 4096, 512], P('rep', 'fsdp')
- moment2_next: bfloat16 [8, 4096, 512], P('rep', 'fsdp')
All inputs are finite; a program needn't handle non-finite values.
Results may differ from a plain program's by a relative error of at most 0.005.
Values may be sent and summed in bfloat16 or wider, within the bound.
No kernel may reach another device: no remote copies, remote signals or barrier semaphores. Data moves between devices by JAX's collectives and lax.ppermute only.
A program may use at most 64 MiB of HBM per device.

v0:
```python
import math

import jax
import jax.numpy as jnp
from jax import lax
from jax.experimental import pallas as pl
from jax.experimental.pallas import tpu as pltpu
from jax.sharding import PartitionSpec as P

LEVELS = 6
CORES = 2
PAD = 16
STRIP = 128
F32 = jnp.float32
BF16 = jnp.bfloat16
ANY = pl.BlockSpec(memory_space=pl.ANY)
HBM = pl.BlockSpec(memory_space=pltpu.HBM)
SMEM = pl.BlockSpec(memory_space=pltpu.SMEM)
VMEM = pl.BlockSpec(memory_space=pltpu.VMEM)
PARAMS = pltpu.CompilerParams(vmem_limit_bytes=16 * 2**20)
OVER_ROWS = (((0,), (0,)), ((), ()))
OVER_COLUMNS = (((1,), (1,)), ((), ()))


def call(kernel, name, **kwargs):
    with jax.named_scope(name):
        return pl.pallas_call(kernel, name=name, compiler_params=PARAMS, **kwargs)


def like(shape, dtype):
    return jax.ShapeDtypeStruct(shape, dtype)


def core_swap(value, name):
    n = lax.axis_size("fsdp")
    with jax.named_scope(name):
        return lax.ppermute(value, "fsdp", [(i, i ^ 1) for i in range(n)])


def chip_shift(value, distance, name):
    n = lax.axis_size("fsdp")
    with jax.named_scope(name):
        return lax.ppermute(value, "fsdp", [(i, (i + CORES * distance) % n) for i in range(n)])


def rep_shift(value, distance, name):
    n = lax.axis_size("rep")
    with jax.named_scope(name):
        return lax.ppermute(value, "rep", [((i - distance) % n, i) for i in range(n)])


def after(value, *done):
    return lax.optimization_barrier((value, *done))[0]


def shard_at(chip_step, other_core):
    n = lax.axis_size("fsdp")
    me = lax.axis_index("fsdp")
    core = lax.rem(me, CORES)
    if other_core:
        core = 1 - core
    return lax.rem(lax.div(me, CORES) + n // CORES - chip_step, n // CORES) * CORES + core


def spans_of(rows, shares, pads=None):
    unit = rows // sum(shares)
    pads = pads or (0,) * len(shares)
    return [(sum(shares[:i]) * unit, share * unit, pads[i]) for i, share in enumerate(shares)]


def strips_of(size):
    return [(at, min(STRIP, size - at)) for at in range(0, size, STRIP)]


def cast_rows(weight, spans, deps):
    kv = weight.shape[1]
    low, high = spans[0][0], sum(spans[-1])

    cuts = [(first + at, high) for first, size in spans for at, high in strips_of(size)]

    def kernel(src, *refs):
        buf, sems = refs[-2:]
        loads = [
            pltpu.make_async_copy(
                src.at[pl.ds(at, high), :], buf.at[pl.ds(at - low, high), :], sems.at[i]
            )
            for i, (at, high) in enumerate(cuts)
        ]
        for load in loads:
            load.start()
        loads = iter(loads)
        for (first, size), out in zip(spans, refs[len(deps) :]):
            for at, high in strips_of(size):
                next(loads).wait()
                here = first - low + at
                out[at : at + high, :] = buf[here : here + high, :].astype(BF16)

    return call(
        kernel,
        "cast",
        in_specs=[ANY] * (1 + len(deps)),
        out_specs=[VMEM] * len(spans),
        out_shape=[like((size, kv), BF16) for _, size in spans],
        scratch_shapes=[pltpu.VMEM((high - low, kv), F32), pltpu.SemaphoreType.DMA((len(cuts),))],
    )(weight, *deps)


def partial_grad(own, sib, cot, cot_sib, chip_step, spans, dtype, deps):
    kv = cot.shape[1]
    tokens = own.shape[0]
    rows = own.shape[1] // lax.axis_size("fsdp")

    def kernel(*refs):
        mine, theirs, cot_ref, cot_sib_ref = refs[:4]
        total = lax.dot_general(mine[...], cot_ref[...], OVER_ROWS, preferred_element_type=F32)
        total += lax.dot_general(theirs[...], cot_sib_ref[...], OVER_ROWS, preferred_element_type=F32)
        for (first, size, pad), out in zip(spans, refs[4 + len(deps) :]):
            out[:size, :] = total[first : first + size, :].astype(dtype)
            if pad:
                out[size:, :] = jnp.zeros((pad, kv), dtype)

    columns = pl.BlockSpec((tokens, rows), lambda g: (0, shard_at(chip_step, False)))
    whole = pl.BlockSpec((tokens, kv), lambda g: (0, 0))
    return call(
        kernel,
        "partial",
        grid=(1,),
        in_specs=[columns, columns, whole, whole] + [ANY] * len(deps),
        out_specs=[pl.BlockSpec((size + pad, kv), lambda g: (0, 0)) for _, size, pad in spans],
        out_shape=[like((size + pad, kv), dtype) for _, size, pad in spans],
    )(own, sib, cot, cot_sib, *deps)


def own_part(own, cot, chip_step):
    kv = cot.shape[1]
    tokens = own.shape[0]
    rows = own.shape[1] // lax.axis_size("fsdp")

    def kernel(mine, cot_ref, out):
        out[...] = lax.dot_general(mine[...], cot_ref[...], OVER_ROWS, preferred_element_type=F32)

    return call(
        kernel,
        "own_part",
        grid=(1,),
        in_specs=[
            pl.BlockSpec((tokens, rows), lambda g: (0, shard_at(chip_step, False))),
            pl.BlockSpec((tokens, kv), lambda g: (0, 0)),
        ],
        out_specs=VMEM,
        out_shape=pltpu.VMEM((rows, kv), F32),
    )(own, cot)


def add_part(begun, sib, cot_sib, chip_step, spans):
    kv = cot_sib.shape[1]
    tokens = sib.shape[0]
    rows = begun.shape[0]

    def kernel(begun_ref, theirs, cot_ref, *outs):
        total = lax.dot_general(theirs[...], cot_ref[...], OVER_ROWS, preferred_element_type=F32)
        for (first, size, _), out in zip(spans, outs):
            here = slice(first, first + size)
            out[...] = (begun_ref[here, :] + total[here, :]).astype(BF16)

    return call(
        kernel,
        "add_part",
        grid=(1,),
        in_specs=[
            VMEM,
            pl.BlockSpec((tokens, rows), lambda g: (0, shard_at(chip_step, False))),
            pl.BlockSpec((tokens, kv), lambda g: (0, 0)),
        ],
        out_specs=[VMEM] * len(spans),
        out_shape=[like((size, kv), BF16) for _, size, _ in spans],
    )(begun, sib, cot_sib)


def own_grad(own, sib, cot, cot_sib, held, step, deps):
    kv = cot.shape[1]
    tokens = own.shape[0]
    rows = own.shape[1] // lax.axis_size("fsdp")
    count = len(held)

    def kernel(*refs):
        step_ref, mine, theirs, cot_ref, cot_sib_ref = refs[:5]
        sources = refs[5 : 5 + count]
        out, scales, *places = refs[5 + count + len(deps) : -1]
        copies = [
            pltpu.make_async_copy(source, place, refs[-1].at[i])
            for i, (source, place) in enumerate(zip(sources, places))
        ]
        for copy in copies:
            copy.start()
        total = lax.dot_general(mine[...], cot_ref[...], OVER_ROWS, preferred_element_type=F32)
        total += lax.dot_general(theirs[...], cot_sib_ref[...], OVER_ROWS, preferred_element_type=F32)
        out[...] = total
        time = jnp.full((8, kv), (step_ref[0] + 1).astype(F32))
        for i, decay in enumerate((0.9, 0.95)):
            scales[8 * i : 8 * (i + 1), :] = 1.0 / (1.0 - jnp.exp(time * math.log(decay)))
        for copy in copies:
            copy.wait()

    columns = pl.BlockSpec((tokens, rows), lambda g: (0, shard_at(0, False)))
    whole = pl.BlockSpec((tokens, kv), lambda g: (0, 0))
    return call(
        kernel,
        "own_grad",
        grid=(1,),
        in_specs=[SMEM, columns, columns, whole, whole] + [ANY] * (count + len(deps)),
        out_specs=[VMEM] * (2 + count),
        out_shape=[pltpu.VMEM((rows, kv), F32), pltpu.VMEM((16, kv), F32)]
        + [pltpu.VMEM(array.shape, array.dtype) for array in held],
        scratch_shapes=[pltpu.SemaphoreType.DMA((count,))],
    )(step.reshape(1), own, sib, cot, cot_sib, *held, *deps)


def adam_rows(span, grad, got, weight, moments, scales, so_far, send, deps):
    first, size, pad = span
    rows, kv = weight.shape
    count = len(got)
    kept = 2 if send else 3
    strips = strips_of(size)

    def kernel(*refs):
        scales_ref, grad_ref = refs[:2]
        got_refs = refs[2 : 2 + count]
        w_ref, m_ref, v_ref = refs[2 + count : 5 + count]
        at = 5 + count + (kept if so_far else 0) + len(deps)
        places = refs[at : at + kept]
        at += kept
        if send:
            up_out, short_out = refs[at : at + 2]
            at += 2
        bufs, sems = refs[at : at + kept], refs[at + kept]
        copies = []
        scale1, scale2 = scales_ref[:1, :], scales_ref[8:9, :]
        for i, (strip, high) in enumerate(strips):
            here = slice(strip, strip + high)
            there = slice(first + strip, first + strip + high)
            g = grad_ref[there, :]
            for ref in got_refs:
                g += ref[here, :].astype(F32)
            w = w_ref[there, :]
            m = 0.9 * m_ref[there, :].astype(F32) + 0.1 * g
            v = 0.95 * v_ref[there, :].astype(F32) + 0.05 * g * g
            up = w - 0.003 * ((m * scale1) / (jnp.sqrt(v * scale2) + 1e-8) + 0.1 * w)
            bufs[0][here, :] = m.astype(BF16)
            bufs[1][here, :] = v.astype(BF16)
            if send:
                up_out[here, :] = up
                short_out[here, :] = up.astype(BF16)
            else:
                bufs[2][here, :] = up
            for j in range(kept):
                copies.append(
                    pltpu.make_async_copy(
                        bufs[j].at[pl.ds(strip, high), :],
                        places[j].at[0, pl.ds(first + strip, high), :],
                        sems.at[j, i],
                    )
                )
                copies[-1].start()
        if send and pad:
            short_out[size:, :] = jnp.zeros((pad, kv), BF16)
        for copy in copies:
            copy.wait()

    kinds = [BF16, BF16] + ([] if send else [F32])
    return call(
        kernel,
        "adam",
        in_specs=[VMEM] * (5 + count) + [HBM] * (kept if so_far else 0) + [ANY] * len(deps),
        out_specs=[HBM] * kept + ([VMEM, VMEM] if send else []),
        out_shape=[pltpu.HBM((1, rows, kv), kind) for kind in kinds]
        + ([like((size, kv), F32), like((size + pad, kv), BF16)] if send else []),
        scratch_shapes=[pltpu.VMEM((size, kv), kind) for kind in kinds]
        + [pltpu.SemaphoreType.DMA((kept, len(strips)))],
        input_output_aliases={5 + count + i: i for i in range(kept)} if so_far else {},
    )(scales, grad, *got, weight, *moments, *(so_far or ()), *deps)


def project(pieces, own, cot, so_far, last, deps, emit=()):
    tokens, width = own.shape
    kv = cot.shape[1]
    shard = width // lax.axis_size("fsdp")
    count = len(pieces)
    sizes = [piece[1] for piece in pieces]

    def kernel(*refs):
        weights, (cot_ref, own_ref) = refs[:count], refs[count : count + 2]
        at = count + 2
        if so_far:
            keys_ref = refs[at]
            at += 2
        at += len(deps)
        keys_out, back_out = refs[at : at + 2]
        spans_out = refs[at + 2 : at + 2 + len(emit)]
        at += 2 + len(emit)
        outs, shorts = refs[at : at + count], refs[at + count : at + count + len(emit)]
        keys_buf, sems = refs[-2:]
        stores = []
        for i, ((first, size), out) in enumerate(zip(emit, spans_out)):
            shorts[i][...] = weights[0][first : first + size, :].astype(BF16)
            stores.append(pltpu.make_async_copy(shorts[i], out, sems.at[count + 1 + i]))
            stores[-1].start()
        total = keys_ref[...] if so_far else None
        for j, (_, _, steps, other, first) in enumerate(pieces):
            place = pl.ds(pl.multiple_of(shard_at(steps, other) * shard + first, 128), sizes[j])
            rows = weights[j][: sizes[j], :].astype(BF16)
            outs[j][...] = lax.dot_general(
                cot_ref[...], rows, OVER_COLUMNS, preferred_element_type=F32
            ).astype(BF16)
            stores.append(pltpu.make_async_copy(outs[j], back_out.at[0, :, place], sems.at[j]))
            stores[-1].start()
            term = jnp.dot(own_ref[:, place], rows, preferred_element_type=F32)
            total = term if total is None else total + term
        if last:
            keys_buf[...] = total.astype(BF16)
            stores.append(pltpu.make_async_copy(keys_buf, keys_out.at[0], sems.at[count]))
            stores[-1].start()
        else:
            keys_out[...] = total
        for store in stores:
            store.wait()

    return call(
        kernel,
        "project",
        in_specs=[VMEM] * (count + 2) + ([VMEM, HBM] if so_far else []) + [ANY] * len(deps),
        out_specs=[HBM if last else VMEM, HBM] + [HBM] * len(emit),
        out_shape=[
            pltpu.HBM((1, tokens, kv), BF16) if last else like((tokens, kv), F32),
            pltpu.HBM((1, tokens, width), BF16),
        ]
        + [pltpu.HBM((size, kv), BF16) for _, size in emit],
        scratch_shapes=[pltpu.VMEM((tokens, size), BF16) for size in sizes]
        + [pltpu.VMEM((size, kv), BF16) for _, size in emit]
        + [pltpu.VMEM((tokens, kv), BF16), pltpu.SemaphoreType.DMA((count + 1 + len(emit),))],
        input_output_aliases={count + 3: 1} if so_far else {},
    )(*[piece[0] for piece in pieces], cot, own, *(so_far or ()), *deps)


def average(rows, spans, updated, neighbours, so_far, deps):
    kv = updated[0].shape[1]
    count = len(spans)
    strips = [(j, first, *strip) for j, (first, size, _) in enumerate(spans) for strip in strips_of(size)]

    def kernel(*refs):
        out, buf, sems = refs[-3:]
        copies = []
        for i, (j, first, strip, high) in enumerate(strips):
            here = slice(strip, strip + high)
            at = pl.ds(first - spans[0][0] + strip, high)
            buf[at, :] = 0.5 * (refs[j][here, :] + refs[count + j][here, :].astype(F32))
            copies.append(
                pltpu.make_async_copy(buf.at[at, :], out.at[0, pl.ds(first + strip, high), :], sems.at[i])
            )
            copies[-1].start()
        for copy in copies:
            copy.wait()

    before = [] if so_far is None else [so_far]
    return call(
        kernel,
        "average",
        in_specs=[VMEM] * (2 * count) + [HBM] * len(before) + [ANY] * len(deps),
        out_specs=HBM,
        out_shape=pltpu.HBM((1, rows, kv), F32),
        scratch_shapes=[
            pltpu.VMEM((sum(size for _, size, _ in spans), kv), F32),
            pltpu.SemaphoreType.DMA((len(strips),)),
        ],
        input_output_aliases={2 * count: 0} if before else {},
    )(*updated, *neighbours, *before, *deps)


def make_branch(distance):
    def branch(hidden, key_grad, weight, moment1, moment2, step):
        chips = lax.axis_size("fsdp") // CORES
        own, cot, w = hidden[0], key_grad[0], weight[0]
        state_in = (w, moment1[0], moment2[0])
        rows = w.shape[0]
        far = range(1, chips)

        def local_pieces(w_sib):
            return [(held[0], rows, 0, False, 0), (w_sib, rows, 0, True, 0)]

        def send_far(part, i):
            return [chip_shift(part, s, f"far{i}") for s in far]

        def pieces_of(i, arrays, order):
            first, size = w_spans[i]
            return [(v, size, s, False, first) for v, s in zip(arrays, far)] + [
                (core_swap(after(v, *order), f"swap{i}"), size, s, True, first) for v, s in zip(arrays, far)
            ]

        def adam(i, state, deps):
            return adam_rows(
                g_spans[i], grad, [got[s][i] for s in far], held[0], held[1:], scales, state, bool(distance), deps
            )

        def partial(s, spans, dtype, deps):
            return partial_grad(own, sib, cot, cot_sib, -s % chips, spans, dtype, deps)

        if 2 * distance >= lax.axis_size("rep"):
            g_spans = spans_of(rows, (20, 19, 25))
            w_spans = [span[:2] for span in spans_of(rows, (3, 3, 2))]
            sib, cot_sib = core_swap(own, "hidden"), core_swap(cot, "cot")
            sent = {s: add_part(own_part(own, cot, -s % chips), sib, cot_sib, -s % chips, g_spans) for s in far}
            got = {s: [chip_shift(part, s, f"grad{i}") for i, part in enumerate(sent[s])] for s in far}
            w_sib = core_swap(after(w, *[sent[s][-1] for s in far]), "w_sib")
            grad, scales, *held = own_grad(own, sib, cot, cot_sib, state_in, step, [sent[s][-1] for s in far])
            keys, back, *parts = project(local_pieces(w_sib), own, cot, None, False, [grad], w_spans)
            there = [send_far(part, i) for i, part in enumerate(parts)]
            state, order, updated, ups, near = None, keys, None, [], []
            for i in range(len(g_spans)):
                if i > 1:
                    updated = order = average(rows, [g_spans[i - 2]], [ups[i - 2]], [near[i - 2]], updated, [order])
                *state, up, order = adam(i, state, [order])
                ups.append(up)
                near.append(rep_shift(order, distance, f"near{i}"))
            updated = average(rows, [g_spans[-2]], [ups[-2]], [near[-2]], updated, [order])
            pieces = [piece for i in range(len(there)) for piece in pieces_of(i, there[i], [updated])]
            keys, back = project(pieces, own, cot, (keys, back), True, [updated])
            updated = average(rows, [g_spans[-1]], [ups[-1]], [near[-1]], updated, [keys])
        elif distance:
            g_spans = spans_of(rows, (25, 20, 19))
            w_spans = [span[:2] for span in spans_of(rows, (2, 3, 3))]
            sent_spans = [(w_spans[i][0], w_spans[i][1] + pad) for i, pad in enumerate((PAD, PAD, 0))]
            sib, cot_sib = core_swap(own, "hidden"), core_swap(cot, "cot")
            (w0,) = cast_rows(w, sent_spans[:1], [])
            there = [send_far(w0, 0)]
            sent = {s: partial(s, g_spans, BF16, [w0]) for s in far}
            got = {s: [chip_shift(part, s, f"grad{i}") for i, part in enumerate(sent[s])] for s in far}
            w_sib = core_swap(after(w, w0), "w_sib")
            grad, scales, *held = own_grad(own, sib, cot, cot_sib, state_in, step, [sent[s][-1] for s in far])
            pieces = local_pieces(w_sib) + pieces_of(0, there[0], [grad])
            keys, back, *parts = project(pieces, own, cot, None, False, [grad], sent_spans[1:])
            there += [send_far(part, 1 + i) for i, part in enumerate(parts)]
            state, order, ups, near = None, keys, [], []
            for i in range(len(g_spans)):
                *state, up, order = adam(i, state, [order])
                ups.append(up)
                near.append(rep_shift(order, distance, f"near{i}"))
            updated = average(rows, g_spans, ups, near, None, [order])
            pieces = pieces_of(1, there[1], [order]) + pieces_of(2, there[2], [updated])
            last = len(far)
            keys, back = project(pieces[:-last], own, cot, (keys, back), False, [updated])
            keys, back = project(pieces[-last:], own, cot, (keys, back), True, [])
        else:
            g_spans = spans_of(rows, (47, 17))
            w_spans = [span[:2] for span in spans_of(rows, (1, 1))]
            sib, w_sib = core_swap(own, "hidden"), core_swap(w, "w_sib")
            parts = cast_rows(w, w_spans, [])
            cot_sib = core_swap(after(cot, parts[0]), "cot")
            there = [send_far(part, i) for i, part in enumerate(parts)]
            sent = {s: partial(s, g_spans, BF16, [parts[0]]) for s in far}
            got = {s: [chip_shift(part, s, f"grad{i}") for i, part in enumerate(sent[s])] for s in far}
            grad, scales, *held = own_grad(own, sib, cot, cot_sib, state_in, step, [sent[s][-1] for s in far])
            keys, back = project(local_pieces(w_sib), own, cot, None, False, [grad])
            pieces = [piece for i in range(len(there)) for piece in pieces_of(i, there[i], [keys])]
            keys, back = project(pieces, own, cot, (keys, back), True, [keys])
            state = adam(0, None, [keys])
            state = adam(1, state, [])
            updated = state[2]
        return keys, back, updated, state[0], state[1]

    return branch


def per_device(hidden, key_grad, weight, moment1, moment2, step):
    replicas = lax.axis_size("rep")
    distances = [2**level % replicas for level in range(LEVELS)]
    kinds = sorted(set(distances))
    level = lax.rem(step, LEVELS)
    pick = jnp.int32(0)
    for i, d in enumerate(distances):
        pick = jnp.where(level == i, kinds.index(d), pick)
    return lax.switch(
        pick, [make_branch(d) for d in kinds], hidden, key_grad, weight, moment1, moment2, step
    )


def solution(mesh):
    spec = P("rep", "fsdp", None)
    return jax.shard_map(
        per_device,
        mesh=mesh,
        in_specs=(spec,) * 5 + (P(),),
        out_specs=(spec,) * 5,
        check_vma=False,
    )
```

profile of v0, /device:TPU:0, one launch (start us, length us, event | category | flops | bytes accessed | tf_op | source)
XLA Modules:
  0.0 54.3 jit_solution(15168106559156009995)
XLA Ops:
  1.3 52.8 %conditional.1 = (bf16[1,256,512]{2,1,0:T(8,128)(2,1)}, bf16[1,256,4096]{2,1,0:T(8,128)(2,1)}, f32[1,1024,512]{2,1,0:T(8,128)}, bf16[1,1024,512]{2,1,0:T(8,128)(2,1)}, bf16[1,1024,512]{2,1,0:T(8,128)(2,1)}) conditional(s32[]{:T(128)} %clamp.3, (f32[1,1024,512]{2,1,0:T(8,128)}, s32[]{:T(128)}, ...), branch_computations={%region_0.1_spmd, %region_1.2_spmd, %region_2.3_spmd, %region_3.4_... | conditional | bytes 65012576 | solution.py:481
  1.3 0.0 copy-start
  1.3 0.5 collective-permute-start.1
  1.9 0.1 collective-permute-start.3
  1.9 1.6 %cast.3 = (bf16[512,512]{1,0:T(8,128)(2,1)S(1)}, bf16[512,512]{1,0:T(8,128)(2,1)S(1)}) custom-call(f32[1024,512]{1,0:T(8,128)} %bitcast.47), custom_call_target="tpu_custom_call" | custom-call | tf_op jit(solution)/shard_map/cond/branch_0_fun/cast/pallas_call | solution.py:98
  3.6 3.0 %collective-permute-start.5 = (bf16[512,512]{1,0:T(8,128)(2,1)S(1)}, bf16[512,512]{1,0:T(8,128)(2,1)S(1)}, u32[]{:S(2)}, u32[]{:S(2)}) collective-permute-start(bf16[512,512]{1,0:T(8,128)(2,1)S(1)} %get-tuple-element.61), channel_id=1, source_target_pairs={{0,2},{1,3},{2,0},{3,1},{4,6},{5,7},{6,4},{7,5},{8,10},{9,11},{10,... | collective-permute-start | bytes 1572872 | tf_op jit(solution)/shard_map/cond/branch_0_fun/far1/ppermute | solution.py:43
  6.6 0.1 collective-permute-start
  6.6 0.1 collective-permute-start.2
  6.7 2.5 %collective-permute-done.2.refs_3_.refs_4_ = bf16[256,512]{1,0:T(8,128)(2,1)S(1)} collective-permute-done((bf16[256,512]{1,0:T(8,128)(2,1)}, bf16[256,512]{1,0:T(8,128)(2,1)S(1)}, u32[]{:S(2)}, u32[]{:S(2)}) %collective-permute-start.2) | collective-permute-done | bytes 262176 | tf_op jit(solution)/shard_map/cond/branch_0_fun/cot/ppermute | solution.py:37
  9.2 1.7 %partial.3 = (bf16[752,512]{1,0:T(8,128)(2,1)S(1)}, bf16[272,512]{1,0:T(8,128)(2,1)S(1)}) custom-call(bf16[256,4096]{1,0:T(8,128)(2,1)S(1)} %bitcast.25, bf16[256,4096]{1,0:T(8,128)(2,1)S(1)} %collective-permute-done.1.refs_1_.refs_2_, bf16[256,512]{1,0:T(8,128)(2,1)} %bitcast.58, bf16[256,512]{1,0:T(8,128)(2,1)S(1)} %collective-permute-done.2.refs_3_.refs_4_, ...), custom_call_target="tpu_custom_call" | custom-call | tf_op jit(solution)/shard_map/cond/branch_0_fun/partial/pallas_call | solution.py:124
  10.9 2.9 %collective-permute-start.8 = (bf16[752,512]{1,0:T(8,128)(2,1)S(1)}, bf16[752,512]{1,0:T(8,128)(2,1)S(1)}, u32[]{:S(2)}, u32[]{:S(2)}) collective-permute-start(bf16[752,512]{1,0:T(8,128)(2,1)S(1)} %get-tuple-element.69), channel_id=1, source_target_pairs={{0,2},{1,3},{2,0},{3,1},{4,6},{5,7},{6,4},{7,5},{8,10},{9,11},{10,... | collective-permute-start | bytes 2310152 | tf_op jit(solution)/shard_map/cond/branch_0_fun/grad0/ppermute | solution.py:43
  13.9 1.8 %own_grad.4 = (f32[1024,512]{1,0:T(8,128)S(1)}, f32[16,512]{1,0:T(8,128)S(1)}, f32[1024,512]{1,0:T(8,128)S(1)}, bf16[1024,512]{1,0:T(8,128)(2,1)S(1)}, bf16[1024,512]{1,0:T(8,128)(2,1)S(1)}) custom-call(s32[1]{0:T(128)} %bitcast.1.refs_0_, bf16[256,4096]{1,0:T(8,128)(2,1)S(1)} %bitcast.26, bf16[256,4096]{1,0:T(8,128)(2,1)S(1)} %collective-permute-done.1.refs_1_.refs_2_, ...), custom_call_target="tpu_custom_call" | custom-call | tf_op jit(solution)/shard_map/cond/branch_0_fun/own_grad/pallas_call | solution.py:207
  15.7 1.7 %project.10 = (f32[256,512]{1,0:T(8,128)S(1)}, bf16[1,256,4096]{2,1,0:T(8,128)(2,1)}) custom-call(f32[1024,512]{1,0:T(8,128)S(1)} %get-tuple-element.57.refs_0_.refs_3_, f32[1024,512]{1,0:T(8,128)S(1)} %collective-permute-done.3.refs_1_, bf16[256,512]{1,0:T(8,128)(2,1)S(1)} %bitcast.60, bf16[256,4096]{1,0:T(8,128)(2,1)S(1)} %bitcast.27, ...), custom_call_target="tpu_custom_call" | custom-call | tf_op jit(solution)/shard_map/cond/branch_0_fun/project/pallas_call | solution.py:328
  17.4 1.9 %collective-permute-done.5.refs_2_ = bf16[512,512]{1,0:T(8,128)(2,1)S(1)} collective-permute-done((bf16[512,512]{1,0:T(8,128)(2,1)S(1)}, bf16[512,512]{1,0:T(8,128)(2,1)S(1)}, u32[]{:S(2)}, u32[]{:S(2)}) %collective-permute-start.5) | collective-permute-done | bytes 524320 | tf_op jit(solution)/shard_map/cond/branch_0_fun/far1/ppermute | solution.py:43
  19.3 11.2 %collective-permute-done.refs_0_ = bf16[512,512]{1,0:T(8,128)(2,1)S(1)} collective-permute-done((bf16[512,512]{1,0:T(8,128)(2,1)S(1)}, bf16[512,512]{1,0:T(8,128)(2,1)S(1)}, u32[]{:S(2)}, u32[]{:S(2)}) %collective-permute-start) | collective-permute-done | bytes 524320 | tf_op jit(solution)/shard_map/cond/branch_0_fun/far0/ppermute | solution.py:43
  30.5 0.0 collective-permute-start.4
  30.5 0.5 collective-permute-start.6
  31.0 2.1 %collective-permute-start.7 = (bf16[272,512]{1,0:T(8,128)(2,1)S(1)}, bf16[272,512]{1,0:T(8,128)(2,1)S(1)}, u32[]{:S(2)}, u32[]{:S(2)}) collective-permute-start(bf16[272,512]{1,0:T(8,128)(2,1)S(1)} %get-tuple-element.56.refs_8_), channel_id=1, source_target_pairs={{0,2},{1,3},{2,0},{3,1},{4,6},{5,7},{6,4},{7,5},{8,10},{9,11},{10,... | collective-permute-start | bytes 835592 | tf_op jit(solution)/shard_map/cond/branch_0_fun/grad1/ppermute | solution.py:43
  33.1 0.1 collective-permute-done.6.refs_3_
  33.2 2.1 %project.11 = (bf16[1,256,512]{2,1,0:T(8,128)(2,1)}, bf16[1,256,4096]{2,1,0:T(8,128)(2,1)}) custom-call(bf16[512,512]{1,0:T(8,128)(2,1)S(1)} %collective-permute-done.refs_0_, bf16[512,512]{1,0:T(8,128)(2,1)S(1)} %collective-permute-done.4.refs_1_, bf16[512,512]{1,0:T(8,128)(2,1)S(1)} %collective-permute-done.5.refs_2_, ...), custom_call_target="tpu_custom_call", output_to_operand_aliasing={{1}: (7, {})} | custom-call | tf_op jit(solution)/shard_map/cond/branch_0_fun/project/pallas_call | solution.py:328
  35.3 11.7 %collective-permute-done.8.refs_2_ = bf16[752,512]{1,0:T(8,128)(2,1)S(1)} collective-permute-done((bf16[752,512]{1,0:T(8,128)(2,1)S(1)}, bf16[752,512]{1,0:T(8,128)(2,1)S(1)}, u32[]{:S(2)}, u32[]{:S(2)}) %collective-permute-start.8) | collective-permute-done | bytes 770080 | tf_op jit(solution)/shard_map/cond/branch_0_fun/grad0/ppermute | solution.py:43
  47.0 2.2 %adam.11 = (bf16[1,1024,512]{2,1,0:T(8,128)(2,1)}, bf16[1,1024,512]{2,1,0:T(8,128)(2,1)}, f32[1,1024,512]{2,1,0:T(8,128)}) custom-call(f32[16,512]{1,0:T(8,128)S(1)} %get-tuple-element.66.refs_0_, f32[1024,512]{1,0:T(8,128)S(1)} %get-tuple-element.58.refs_4_.refs_1_, bf16[752,512]{1,0:T(8,128)(2,1)S(1)} %collective-permute-done.8.refs_2_, ...), custom_call_target="tpu_custom_call" | custom-call | tf_op jit(solution)/shard_map/cond/branch_0_fun/adam/pallas_call | solution.py:271
  49.3 3.1 %collective-permute-done.7.refs_2_ = bf16[272,512]{1,0:T(8,128)(2,1)S(1)} collective-permute-done((bf16[272,512]{1,0:T(8,128)(2,1)S(1)}, bf16[272,512]{1,0:T(8,128)(2,1)S(1)}, u32[]{:S(2)}, u32[]{:S(2)}) %collective-permute-start.7) | collective-permute-done | bytes 278560 | tf_op jit(solution)/shard_map/cond/branch_0_fun/grad1/ppermute | solution.py:43
  52.4 1.3 %adam.12 = (bf16[1,1024,512]{2,1,0:T(8,128)(2,1)}, bf16[1,1024,512]{2,1,0:T(8,128)(2,1)}, f32[1,1024,512]{2,1,0:T(8,128)}) custom-call(f32[16,512]{1,0:T(8,128)S(1)} %get-tuple-element.66.refs_0_, f32[1024,512]{1,0:T(8,128)S(1)} %get-tuple-element.58.refs_4_.refs_1_, ...), custom_call_target="tpu_custom_call", output_to_operand_aliasing={{0}: (6, {}), {1}: (7, {}), {2}: (8, {})} | custom-call | tf_op jit(solution)/shard_map/cond/branch_0_fun/adam/pallas_call | solution.py:271
  (12 shorter events, 0.0 us)
Async XLA Ops:
  1.3 7.9 %copy-start = (bf16[1,256,4096]{2,1,0:T(8,128)(2,1)S(1)}, bf16[1,256,4096]{2,1,0:T(8,128)(2,1)}, u32[]{:S(2)}) copy-start(bf16[1,256,4096]{2,1,0:T(8,128)(2,1)} %get-tuple-element.51) | copy-start | bytes 6291460 | tf_op jit(solution)/shard_map/cond
  1.3 7.9 %collective-permute-start.1 = (bf16[256,4096]{1,0:T(8,128)(2,1)}, bf16[256,4096]{1,0:T(8,128)(2,1)S(1)}, u32[]{:S(2)}, u32[]{:S(2)}) collective-permute-start(bf16[256,4096]{1,0:T(8,128)(2,1)} %bitcast.24), channel_id=1, source_target_pairs={{0,1},{1,0},{2,3},{3,2},{4,5},{5,4},{6,7},{7,6},{8,9},{9,8},{10,11... | collective-permute-start | bytes 6291464 | tf_op jit(solution)/shard_map/cond/branch_0_fun/hidden/ppermute | solution.py:37
  1.9 13.8 %collective-permute-start.3 = (f32[1024,512]{1,0:T(8,128)}, f32[1024,512]{1,0:T(8,128)S(1)}, u32[]{:S(2)}, u32[]{:S(2)}) collective-permute-start(f32[1024,512]{1,0:T(8,128)} %bitcast.46), channel_id=1, source_target_pairs={{0,1},{1,0},{2,3},{3,2},{4,5},{5,4},{6,7},{7,6},{8,9},{9,8},{10,11... | collective-permute-start | bytes 6291464 | tf_op jit(solution)/shard_map/cond/branch_0_fun/w_sib/ppermute | solution.py:37
  3.6 15.7 %collective-permute-start.5 = (bf16[512,512]{1,0:T(8,128)(2,1)S(1)}, bf16[512,512]{1,0:T(8,128)(2,1)S(1)}, u32[]{:S(2)}, u32[]{:S(2)}) collective-permute-start(bf16[512,512]{1,0:T(8,128)(2,1)S(1)} %get-tuple-element.61), channel_id=1, source_target_pairs={{0,2},{1,3},{2,0},{3,1},{4,6},{5,7},{6,4},{7,5},{8,10},{9,11},{10,... | collective-permute-start | bytes 1572872 | tf_op jit(solution)/shard_map/cond/branch_0_fun/far1/ppermute | solution.py:43
  6.6 24.0 %collective-permute-start = (bf16[512,512]{1,0:T(8,128)(2,1)S(1)}, bf16[512,512]{1,0:T(8,128)(2,1)S(1)}, u32[]{:S(2)}, u32[]{:S(2)}) collective-permute-start(bf16[512,512]{1,0:T(8,128)(2,1)S(1)} %get-tuple-element.49.refs_4_), channel_id=1, source_target_pairs={{0,2},{1,3},{2,0},{3,1},{4,6},{5,7},{6,4},{7,5},{8,10},{9,11},{10,... | collective-permute-start | bytes 1572872 | tf_op jit(solution)/shard_map/cond/branch_0_fun/far0/ppermute | solution.py:43
  6.6 7.2 %copy-start.4 = (f32[1,1024,512]{2,1,0:T(8,128)S(1)}, f32[1,1024,512]{2,1,0:T(8,128)}, u32[]{:S(2)}) copy-start(f32[1,1024,512]{2,1,0:T(8,128)} %get-tuple-element.48) | copy-start | bytes 6291460 | tf_op jit(solution)/shard_map/cond
  6.6 7.2 %copy-start.8 = (bf16[1,256,512]{2,1,0:T(8,128)(2,1)S(1)}, bf16[1,256,512]{2,1,0:T(8,128)(2,1)}, u32[]{:S(2)}) copy-start(bf16[1,256,512]{2,1,0:T(8,128)(2,1)} %get-tuple-element.52) | copy-start | bytes 786436 | tf_op jit(solution)/shard_map/cond
  6.6 7.2 %copy-start.12 = (bf16[1,1024,512]{2,1,0:T(8,128)(2,1)S(1)}, bf16[1,1024,512]{2,1,0:T(8,128)(2,1)}, u32[]{:S(2)}) copy-start(bf16[1,1024,512]{2,1,0:T(8,128)(2,1)} %get-tuple-element.54) | copy-start | bytes 3145732 | tf_op jit(solution)/shard_map/cond
  6.6 7.2 %copy-start.16 = (bf16[1,1024,512]{2,1,0:T(8,128)(2,1)S(1)}, bf16[1,1024,512]{2,1,0:T(8,128)(2,1)}, u32[]{:S(2)}) copy-start(bf16[1,1024,512]{2,1,0:T(8,128)(2,1)} %get-tuple-element.55) | copy-start | bytes 3145732 | tf_op jit(solution)/shard_map/cond
  6.6 2.6 %collective-permute-start.2 = (bf16[256,512]{1,0:T(8,128)(2,1)}, bf16[256,512]{1,0:T(8,128)(2,1)S(1)}, u32[]{:S(2)}, u32[]{:S(2)}) collective-permute-start(bf16[256,512]{1,0:T(8,128)(2,1)} %bitcast.57), channel_id=1, source_target_pairs={{0,1},{1,0},{2,3},{3,2},{4,5},{5,4},{6,7},{7,6},{8,9},{9,8},{10,11... | collective-permute-start | bytes 786440 | tf_op jit(solution)/shard_map/cond/branch_0_fun/cot/ppermute | solution.py:37
  10.9 36.1 %collective-permute-start.8 = (bf16[752,512]{1,0:T(8,128)(2,1)S(1)}, bf16[752,512]{1,0:T(8,128)(2,1)S(1)}, u32[]{:S(2)}, u32[]{:S(2)}) collective-permute-start(bf16[752,512]{1,0:T(8,128)(2,1)S(1)} %get-tuple-element.69), channel_id=1, source_target_pairs={{0,2},{1,3},{2,0},{3,1},{4,6},{5,7},{6,4},{7,5},{8,10},{9,11},{10,... | collective-permute-start | bytes 2310152 | tf_op jit(solution)/shard_map/cond/branch_0_fun/grad0/ppermute | solution.py:43
  30.5 2.6 %collective-permute-start.4 = (bf16[512,512]{1,0:T(8,128)(2,1)S(1)}, bf16[512,512]{1,0:T(8,128)(2,1)S(1)}, u32[]{:S(2)}, u32[]{:S(2)}) collective-permute-start(bf16[512,512]{1,0:T(8,128)(2,1)S(1)} %collective-permute-done.refs_0_), channel_id=1, source_target_pairs={{0,1},{1,0},{2,3},{3,2},{4,5},{5,4},{6,7},{7,6},{8,9},{9,8},{10,11... | collective-permute-start | bytes 1572872 | tf_op jit(solution)/shard_map/cond/branch_0_fun/swap0/ppermute | solution.py:37
  30.5 2.7 %collective-permute-start.6 = (bf16[512,512]{1,0:T(8,128)(2,1)S(1)}, bf16[512,512]{1,0:T(8,128)(2,1)S(1)}, u32[]{:S(2)}, u32[]{:S(2)}) collective-permute-start(bf16[512,512]{1,0:T(8,128)(2,1)S(1)} %collective-permute-done.5.refs_2_), channel_id=1, source_target_pairs={{0,1},{1,0},{2,3},{3,2},{4,5},{5,4},{6,7},{7,6},{8,9},{9,8},{10,11... | collective-permute-start | bytes 1572872 | tf_op jit(solution)/shard_map/cond/branch_0_fun/swap1/ppermute | solution.py:37
  31.0 21.4 %collective-permute-start.7 = (bf16[272,512]{1,0:T(8,128)(2,1)S(1)}, bf16[272,512]{1,0:T(8,128)(2,1)S(1)}, u32[]{:S(2)}, u32[]{:S(2)}) collective-permute-start(bf16[272,512]{1,0:T(8,128)(2,1)S(1)} %get-tuple-element.56.refs_8_), channel_id=1, source_target_pairs={{0,2},{1,3},{2,0},{3,1},{4,6},{5,7},{6,4},{7,5},{8,10},{9,11},{10,... | collective-permute-start | bytes 835592 | tf_op jit(solution)/shard_map/cond/branch_0_fun/grad1/ppermute | solution.py:43
where the time goes:
time: 54.5 us; the launch traced here: 54.3 us
  waiting for transfers between devices  30.6 us (56%)
  Pallas kernels  12.4 us (23%)
  starting transfers between devices  9.24 us (17%)
  between operations  1.51 us (3%)
  loops' own time  0.56 us (1%)
    ppermute x4, waiting for transfers between devices, chip_shift(): lax.ppermute(value, 'fsdp', [(i, (i + CORES * distance) % n) for i in ran...  28 us
    ppermute x4, starting transfers between devices, chip_shift(): lax.ppermute(value, 'fsdp', [(i, (i + CORES * distance) % n) for i in ran...  8.06 us
    pallas_call x2, Pallas kernels, project(): call(kernel, 'project', in_specs=[VMEM] * (count + 2) + ([VMEM, HBM] if s...  3.83 us
    pallas_call x2, Pallas kernels, adam_rows(): call(kernel, 'adam', in_specs=[VMEM] * (5 + count) + [HBM] * (kept if so_...  3.52 us
    ppermute x5, waiting for transfers between devices, core_swap(): return lax.ppermute(value, 'fsdp', [(i, i ^ 1) for i in range(n)])  2.6 us
    pallas_call x1, Pallas kernels, own_grad(): call(kernel, 'own_grad', grid=(1,), in_specs=[SMEM, columns, columns, who...  1.79 us
    pallas_call x1, Pallas kernels, partial_grad(): call(kernel, 'partial', grid=(1,), in_specs=[columns, columns, whole, who...  1.68 us
    pallas_call x1, Pallas kernels, cast_rows(): call(kernel, 'cast', in_specs=[ANY] * (1 + len(deps)), out_specs=[VMEM] *...  1.62 us
  transfers between devices with their start and end apart: 9, of which 6 were waited for; matrix products, arithmetic and copies ran while one was open for 0% of the time, Pallas kernels for 21%

commit v1 on v0

--- a/solution.py
+++ b/solution.py
@@ -444,11 +444,13 @@
                 *state, up, order = adam(i, state, [order])
                 ups.append(up)
                 near.append(rep_shift(order, distance, f"near{i}"))
-            updated = average(rows, g_spans, ups, near, None, [order])
-            pieces = pieces_of(1, there[1], [order]) + pieces_of(2, there[2], [updated])
-            last = len(far)
-            keys, back = project(pieces[:-last], own, cot, (keys, back), False, [updated])
-            keys, back = project(pieces[-last:], own, cot, (keys, back), True, [])
+            here = len(far)
+            pieces = pieces_of(1, there[1], [order])
+            keys, back = project(pieces[:here], own, cot, (keys, back), False, [order])
+            updated = average(rows, g_spans, ups, near, None, [keys])
+            pieces = pieces[here:] + pieces_of(2, there[2], [updated])
+            keys, back = project(pieces[:-here], own, cot, (keys, back), False, [updated])
+            keys, back = project(pieces[-here:], own, cot, (keys, back), True, [])
         else:
             g_spans = spans_of(rows, (47, 17))
             w_spans = [span[:2] for span in spans_of(rows, (1, 1))]

time: 54.5 us -> 54.6 us (level)
  no operation moved by 1% of the time
where the time goes in v1:
time: 54.6 us; the launch traced here: 54.4 us
  waiting for transfers between devices  30.6 us (56%)
  Pallas kernels  12.4 us (23%)
  starting transfers between devices  9.24 us (17%)
  between operations  1.53 us (3%)
  loops' own time  0.64 us (1%)
    ppermute x4, waiting for transfers between devices, chip_shift(): lax.ppermute(value, 'fsdp', [(i, (i + CORES * distance) % n) for i in ran...  28 us
    ppermute x4, starting transfers between devices, chip_shift(): lax.ppermute(value, 'fsdp', [(i, (i + CORES * distance) % n) for i in ran...  8.06 us
    pallas_call x2, Pallas kernels, project(): call(kernel, 'project', in_specs=[VMEM] * (count + 2) + ([VMEM, HBM] if s...  3.83 us
    pallas_call x2, Pallas kernels, adam_rows(): call(kernel, 'adam', in_specs=[VMEM] * (5 + count) + [HBM] * (kept if so_...  3.52 us
    ppermute x5, waiting for transfers between devices, core_swap(): return lax.ppermute(value, 'fsdp', [(i, i ^ 1) for i in range(n)])  2.6 us
    pallas_call x1, Pallas kernels, own_grad(): call(kernel, 'own_grad', grid=(1,), in_specs=[SMEM, columns, columns, who...  1.79 us
    pallas_call x1, Pallas kernels, partial_grad(): call(kernel, 'partial', grid=(1,), in_specs=[columns, columns, whole, who...  1.68 us
    pallas_call x1, Pallas kernels, cast_rows(): call(kernel, 'cast', in_specs=[ANY] * (1 + len(deps)), out_specs=[VMEM] *...  1.62 us
  transfers between devices with their start and end apart: 9, of which 6 were waited for; matrix products, arithmetic and copies ran while one was open for 0% of the time, Pallas kernels for 21%

profile of v1, /device:TPU:0, one launch (start us, length us, event | category | flops | bytes accessed | tf_op | source)
XLA Modules:
  0.0 54.4 jit_solution(1208555286047979877)
XLA Ops:
  1.3 52.9 %conditional.1 = (bf16[1,256,512]{2,1,0:T(8,128)(2,1)}, bf16[1,256,4096]{2,1,0:T(8,128)(2,1)}, f32[1,1024,512]{2,1,0:T(8,128)}, bf16[1,1024,512]{2,1,0:T(8,128)(2,1)}, bf16[1,1024,512]{2,1,0:T(8,128)(2,1)}) conditional(s32[]{:T(128)} %clamp.3, (f32[1,1024,512]{2,1,0:T(8,128)}, s32[]{:T(128)}, ...), branch_computations={%region_0.1_spmd, %region_1.2_spmd, %region_2.3_spmd, %region_3.4_... | conditional | bytes 65012576 | solution.py:483
  1.3 0.0 copy-start
  1.3 0.5 collective-permute-start.1
  1.9 0.1 collective-permute-start.3
  1.9 1.6 %cast.3 = (bf16[512,512]{1,0:T(8,128)(2,1)S(1)}, bf16[512,512]{1,0:T(8,128)(2,1)S(1)}) custom-call(f32[1024,512]{1,0:T(8,128)} %bitcast.73), custom_call_target="tpu_custom_call" | custom-call | tf_op jit(solution)/shard_map/cond/branch_0_fun/cast/pallas_call | solution.py:98
  3.6 3.0 %collective-permute-start.5 = (bf16[512,512]{1,0:T(8,128)(2,1)S(1)}, bf16[512,512]{1,0:T(8,128)(2,1)S(1)}, u32[]{:S(2)}, u32[]{:S(2)}) collective-permute-start(bf16[512,512]{1,0:T(8,128)(2,1)S(1)} %get-tuple-element.61), channel_id=1, source_target_pairs={{0,2},{1,3},{2,0},{3,1},{4,6},{5,7},{6,4},{7,5},{8,10},{9,11},{10,... | collective-permute-start | bytes 1572872 | tf_op jit(solution)/shard_map/cond/branch_0_fun/far1/ppermute | solution.py:43
  6.6 0.1 collective-permute-start
  6.6 0.1 collective-permute-start.2
  6.7 2.5 %collective-permute-done.2.refs_3_.refs_4_ = bf16[256,512]{1,0:T(8,128)(2,1)S(1)} collective-permute-done((bf16[256,512]{1,0:T(8,128)(2,1)}, bf16[256,512]{1,0:T(8,128)(2,1)S(1)}, u32[]{:S(2)}, u32[]{:S(2)}) %collective-permute-start.2) | collective-permute-done | bytes 262176 | tf_op jit(solution)/shard_map/cond/branch_0_fun/cot/ppermute | solution.py:37
  9.2 1.7 %partial.3 = (bf16[752,512]{1,0:T(8,128)(2,1)S(1)}, bf16[272,512]{1,0:T(8,128)(2,1)S(1)}) custom-call(bf16[256,4096]{1,0:T(8,128)(2,1)S(1)} %bitcast.25, bf16[256,4096]{1,0:T(8,128)(2,1)S(1)} %collective-permute-done.1.refs_1_.refs_2_, bf16[256,512]{1,0:T(8,128)(2,1)} %bitcast.49, bf16[256,512]{1,0:T(8,128)(2,1)S(1)} %collective-permute-done.2.refs_3_.refs_4_, ...), custom_call_target="tpu_custom_call" | custom-call | tf_op jit(solution)/shard_map/cond/branch_0_fun/partial/pallas_call | solution.py:124
  10.9 2.9 %collective-permute-start.8 = (bf16[752,512]{1,0:T(8,128)(2,1)S(1)}, bf16[752,512]{1,0:T(8,128)(2,1)S(1)}, u32[]{:S(2)}, u32[]{:S(2)}) collective-permute-start(bf16[752,512]{1,0:T(8,128)(2,1)S(1)} %get-tuple-element.69), channel_id=1, source_target_pairs={{0,2},{1,3},{2,0},{3,1},{4,6},{5,7},{6,4},{7,5},{8,10},{9,11},{10,... | collective-permute-start | bytes 2310152 | tf_op jit(solution)/shard_map/cond/branch_0_fun/grad0/ppermute | solution.py:43
  13.9 1.8 %own_grad.4 = (f32[1024,512]{1,0:T(8,128)S(1)}, f32[16,512]{1,0:T(8,128)S(1)}, f32[1024,512]{1,0:T(8,128)S(1)}, bf16[1024,512]{1,0:T(8,128)(2,1)S(1)}, bf16[1024,512]{1,0:T(8,128)(2,1)S(1)}) custom-call(s32[1]{0:T(128)} %bitcast.1.refs_0_, bf16[256,4096]{1,0:T(8,128)(2,1)S(1)} %bitcast.26, bf16[256,4096]{1,0:T(8,128)(2,1)S(1)} %collective-permute-done.1.refs_1_.refs_2_, ...), custom_call_target="tpu_custom_call" | custom-call | tf_op jit(solution)/shard_map/cond/branch_0_fun/own_grad/pallas_call | solution.py:207
  15.7 1.7 %project.12 = (f32[256,512]{1,0:T(8,128)S(1)}, bf16[1,256,4096]{2,1,0:T(8,128)(2,1)}) custom-call(f32[1024,512]{1,0:T(8,128)S(1)} %get-tuple-element.57.refs_0_.refs_3_, f32[1024,512]{1,0:T(8,128)S(1)} %collective-permute-done.3.refs_1_, bf16[256,512]{1,0:T(8,128)(2,1)S(1)} %bitcast.51, bf16[256,4096]{1,0:T(8,128)(2,1)S(1)} %bitcast.27, ...), custom_call_target="tpu_custom_call" | custom-call | tf_op jit(solution)/shard_map/cond/branch_0_fun/project/pallas_call | solution.py:328
  17.4 1.9 %collective-permute-done.5.refs_2_ = bf16[512,512]{1,0:T(8,128)(2,1)S(1)} collective-permute-done((bf16[512,512]{1,0:T(8,128)(2,1)S(1)}, bf16[512,512]{1,0:T(8,128)(2,1)S(1)}, u32[]{:S(2)}, u32[]{:S(2)}) %collective-permute-start.5) | collective-permute-done | bytes 524320 | tf_op jit(solution)/shard_map/cond/branch_0_fun/far1/ppermute | solution.py:43
  19.3 11.2 %collective-permute-done.refs_0_ = bf16[512,512]{1,0:T(8,128)(2,1)S(1)} collective-permute-done((bf16[512,512]{1,0:T(8,128)(2,1)S(1)}, bf16[512,512]{1,0:T(8,128)(2,1)S(1)}, u32[]{:S(2)}, u32[]{:S(2)}) %collective-permute-start) | collective-permute-done | bytes 524320 | tf_op jit(solution)/shard_map/cond/branch_0_fun/far0/ppermute | solution.py:43
  30.5 0.0 collective-permute-start.4
  30.5 0.5 collective-permute-start.6
  31.0 2.1 %collective-permute-start.7 = (bf16[272,512]{1,0:T(8,128)(2,1)S(1)}, bf16[272,512]{1,0:T(8,128)(2,1)S(1)}, u32[]{:S(2)}, u32[]{:S(2)}) collective-permute-start(bf16[272,512]{1,0:T(8,128)(2,1)S(1)} %get-tuple-element.56.refs_8_), channel_id=1, source_target_pairs={{0,2},{1,3},{2,0},{3,1},{4,6},{5,7},{6,4},{7,5},{8,10},{9,11},{10,... | collective-permute-start | bytes 835592 | tf_op jit(solution)/shard_map/cond/branch_0_fun/grad1/ppermute | solution.py:43
  33.1 0.1 collective-permute-done.6.refs_3_
  33.2 2.1 %project.13 = (bf16[1,256,512]{2,1,0:T(8,128)(2,1)}, bf16[1,256,4096]{2,1,0:T(8,128)(2,1)}) custom-call(bf16[512,512]{1,0:T(8,128)(2,1)S(1)} %collective-permute-done.refs_0_, bf16[512,512]{1,0:T(8,128)(2,1)S(1)} %collective-permute-done.4.refs_1_, bf16[512,512]{1,0:T(8,128)(2,1)S(1)} %collective-permute-done.5.refs_2_, ...), custom_call_target="tpu_custom_call", output_to_operand_aliasing={{1}: (7, {})} | custom-call | tf_op jit(solution)/shard_map/cond/branch_0_fun/project/pallas_call | solution.py:328
  35.3 11.7 %collective-permute-done.8.refs_2_ = bf16[752,512]{1,0:T(8,128)(2,1)S(1)} collective-permute-done((bf16[752,512]{1,0:T(8,128)(2,1)S(1)}, bf16[752,512]{1,0:T(8,128)(2,1)S(1)}, u32[]{:S(2)}, u32[]{:S(2)}) %collective-permute-start.8) | collective-permute-done | bytes 770080 | tf_op jit(solution)/shard_map/cond/branch_0_fun/grad0/ppermute | solution.py:43
  47.0 2.2 %adam.11 = (bf16[1,1024,512]{2,1,0:T(8,128)(2,1)}, bf16[1,1024,512]{2,1,0:T(8,128)(2,1)}, f32[1,1024,512]{2,1,0:T(8,128)}) custom-call(f32[16,512]{1,0:T(8,128)S(1)} %get-tuple-element.66.refs_0_, f32[1024,512]{1,0:T(8,128)S(1)} %get-tuple-element.58.refs_4_.refs_1_, bf16[752,512]{1,0:T(8,128)(2,1)S(1)} %collective-permute-done.8.refs_2_, ...), custom_call_target="tpu_custom_call" | custom-call | tf_op jit(solution)/shard_map/cond/branch_0_fun/adam/pallas_call | solution.py:271
  49.3 3.1 %collective-permute-done.7.refs_2_ = bf16[272,512]{1,0:T(8,128)(2,1)S(1)} collective-permute-done((bf16[272,512]{1,0:T(8,128)(2,1)S(1)}, bf16[272,512]{1,0:T(8,128)(2,1)S(1)}, u32[]{:S(2)}, u32[]{:S(2)}) %collective-permute-start.7) | collective-permute-done | bytes 278560 | tf_op jit(solution)/shard_map/cond/branch_0_fun/grad1/ppermute | solution.py:43
  52.4 1.3 %adam.12 = (bf16[1,1024,512]{2,1,0:T(8,128)(2,1)}, bf16[1,1024,512]{2,1,0:T(8,128)(2,1)}, f32[1,1024,512]{2,1,0:T(8,128)}) custom-call(f32[16,512]{1,0:T(8,128)S(1)} %get-tuple-element.66.refs_0_, f32[1024,512]{1,0:T(8,128)S(1)} %get-tuple-element.58.refs_4_.refs_1_, ...), custom_call_target="tpu_custom_call", output_to_operand_aliasing={{0}: (6, {}), {1}: (7, {}), {2}: (8, {})} | custom-call | tf_op jit(solution)/shard_map/cond/branch_0_fun/adam/pallas_call | solution.py:271
  (12 shorter events, 0.0 us)
Async XLA Ops:
  1.3 7.9 %copy-start = (bf16[1,256,4096]{2,1,0:T(8,128)(2,1)S(1)}, bf16[1,256,4096]{2,1,0:T(8,128)(2,1)}, u32[]{:S(2)}) copy-start(bf16[1,256,4096]{2,1,0:T(8,128)(2,1)} %get-tuple-element.51) | copy-start | bytes 6291460 | tf_op jit(solution)/shard_map/cond
  1.3 7.9 %collective-permute-start.1 = (bf16[256,4096]{1,0:T(8,128)(2,1)}, bf16[256,4096]{1,0:T(8,128)(2,1)S(1)}, u32[]{:S(2)}, u32[]{:S(2)}) collective-permute-start(bf16[256,4096]{1,0:T(8,128)(2,1)} %bitcast.24), channel_id=1, source_target_pairs={{0,1},{1,0},{2,3},{3,2},{4,5},{5,4},{6,7},{7,6},{8,9},{9,8},{10,11... | collective-permute-start | bytes 6291464 | tf_op jit(solution)/shard_map/cond/branch_0_fun/hidden/ppermute | solution.py:37
  1.9 13.8 %collective-permute-start.3 = (f32[1024,512]{1,0:T(8,128)}, f32[1024,512]{1,0:T(8,128)S(1)}, u32[]{:S(2)}, u32[]{:S(2)}) collective-permute-start(f32[1024,512]{1,0:T(8,128)} %bitcast.72), channel_id=1, source_target_pairs={{0,1},{1,0},{2,3},{3,2},{4,5},{5,4},{6,7},{7,6},{8,9},{9,8},{10,11... | collective-permute-start | bytes 6291464 | tf_op jit(solution)/shard_map/cond/branch_0_fun/w_sib/ppermute | solution.py:37
  3.6 15.7 %collective-permute-start.5 = (bf16[512,512]{1,0:T(8,128)(2,1)S(1)}, bf16[512,512]{1,0:T(8,128)(2,1)S(1)}, u32[]{:S(2)}, u32[]{:S(2)}) collective-permute-start(bf16[512,512]{1,0:T(8,128)(2,1)S(1)} %get-tuple-element.61), channel_id=1, source_target_pairs={{0,2},{1,3},{2,0},{3,1},{4,6},{5,7},{6,4},{7,5},{8,10},{9,11},{10,... | collective-permute-start | bytes 1572872 | tf_op jit(solution)/shard_map/cond/branch_0_fun/far1/ppermute | solution.py:43
  6.6 24.0 %collective-permute-start = (bf16[512,512]{1,0:T(8,128)(2,1)S(1)}, bf16[512,512]{1,0:T(8,128)(2,1)S(1)}, u32[]{:S(2)}, u32[]{:S(2)}) collective-permute-start(bf16[512,512]{1,0:T(8,128)(2,1)S(1)} %get-tuple-element.49.refs_4_), channel_id=1, source_target_pairs={{0,2},{1,3},{2,0},{3,1},{4,6},{5,7},{6,4},{7,5},{8,10},{9,11},{10,... | collective-permute-start | bytes 1572872 | tf_op jit(solution)/shard_map/cond/branch_0_fun/far0/ppermute | solution.py:43
  6.6 7.2 %copy-start.4 = (bf16[1,256,512]{2,1,0:T(8,128)(2,1)S(1)}, bf16[1,256,512]{2,1,0:T(8,128)(2,1)}, u32[]{:S(2)}) copy-start(bf16[1,256,512]{2,1,0:T(8,128)(2,1)} %get-tuple-element.52) | copy-start | bytes 786436 | tf_op jit(solution)/shard_map/cond
  6.6 7.2 %copy-start.8 = (f32[1,1024,512]{2,1,0:T(8,128)S(1)}, f32[1,1024,512]{2,1,0:T(8,128)}, u32[]{:S(2)}) copy-start(f32[1,1024,512]{2,1,0:T(8,128)} %get-tuple-element.48) | copy-start | bytes 6291460 | tf_op jit(solution)/shard_map/cond
  6.6 7.2 %copy-start.12 = (bf16[1,1024,512]{2,1,0:T(8,128)(2,1)S(1)}, bf16[1,1024,512]{2,1,0:T(8,128)(2,1)}, u32[]{:S(2)}) copy-start(bf16[1,1024,512]{2,1,0:T(8,128)(2,1)} %get-tuple-element.54) | copy-start | bytes 3145732 | tf_op jit(solution)/shard_map/cond
  6.6 7.2 %copy-start.16 = (bf16[1,1024,512]{2,1,0:T(8,128)(2,1)S(1)}, bf16[1,1024,512]{2,1,0:T(8,128)(2,1)}, u32[]{:S(2)}) copy-start(bf16[1,1024,512]{2,1,0:T(8,128)(2,1)} %get-tuple-element.55) | copy-start | bytes 3145732 | tf_op jit(solution)/shard_map/cond
  6.6 2.6 %collective-permute-start.2 = (bf16[256,512]{1,0:T(8,128)(2,1)}, bf16[256,512]{1,0:T(8,128)(2,1)S(1)}, u32[]{:S(2)}, u32[]{:S(2)}) collective-permute-start(bf16[256,512]{1,0:T(8,128)(2,1)} %bitcast.48), channel_id=1, source_target_pairs={{0,1},{1,0},{2,3},{3,2},{4,5},{5,4},{6,7},{7,6},{8,9},{9,8},{10,11... | collective-permute-start | bytes 786440 | tf_op jit(solution)/shard_map/cond/branch_0_fun/cot/ppermute | solution.py:37
  10.9 36.1 %collective-permute-start.8 = (bf16[752,512]{1,0:T(8,128)(2,1)S(1)}, bf16[752,512]{1,0:T(8,128)(2,1)S(1)}, u32[]{:S(2)}, u32[]{:S(2)}) collective-permute-start(bf16[752,512]{1,0:T(8,128)(2,1)S(1)} %get-tuple-element.69), channel_id=1, source_target_pairs={{0,2},{1,3},{2,0},{3,1},{4,6},{5,7},{6,4},{7,5},{8,10},{9,11},{10,... | collective-permute-start | bytes 2310152 | tf_op jit(solution)/shard_map/cond/branch_0_fun/grad0/ppermute | solution.py:43
  30.5 2.6 %collective-permute-start.4 = (bf16[512,512]{1,0:T(8,128)(2,1)S(1)}, bf16[512,512]{1,0:T(8,128)(2,1)S(1)}, u32[]{:S(2)}, u32[]{:S(2)}) collective-permute-start(bf16[512,512]{1,0:T(8,128)(2,1)S(1)} %collective-permute-done.refs_0_), channel_id=1, source_target_pairs={{0,1},{1,0},{2,3},{3,2},{4,5},{5,4},{6,7},{7,6},{8,9},{9,8},{10,11... | collective-permute-start | bytes 1572872 | tf_op jit(solution)/shard_map/cond/branch_0_fun/swap0/ppermute | solution.py:37
  30.5 2.7 %collective-permute-start.6 = (bf16[512,512]{1,0:T(8,128)(2,1)S(1)}, bf16[512,512]{1,0:T(8,128)(2,1)S(1)}, u32[]{:S(2)}, u32[]{:S(2)}) collective-permute-start(bf16[512,512]{1,0:T(8,128)(2,1)S(1)} %collective-permute-done.5.refs_2_), channel_id=1, source_target_pairs={{0,1},{1,0},{2,3},{3,2},{4,5},{5,4},{6,7},{7,6},{8,9},{9,8},{10,11... | collective-permute-start | bytes 1572872 | tf_op jit(solution)/shard_map/cond/branch_0_fun/swap1/ppermute | solution.py:37
  31.0 21.4 %collective-permute-start.7 = (bf16[272,512]{1,0:T(8,128)(2,1)S(1)}, bf16[272,512]{1,0:T(8,128)(2,1)S(1)}, u32[]{:S(2)}, u32[]{:S(2)}) collective-permute-start(bf16[272,512]{1,0:T(8,128)(2,1)S(1)} %get-tuple-element.56.refs_8_), channel_id=1, source_target_pairs={{0,2},{1,3},{2,0},{3,1},{4,6},{5,7},{6,4},{7,5},{8,10},{9,11},{10,... | collective-permute-start | bytes 835592 | tf_op jit(solution)/shard_map/cond/branch_0_fun/grad1/ppermute | solution.py:43
